TPU v7x, 512 devices: a whole 4x4x16 slice. The times are simulated.
512 devices in a mesh: dp: 4 (over x), expert: 128 (over z, y, core).
Axes of the slice: x: 4, y: 4, z: 16, core: 2. Of those that a mesh axis runs over, the one named last changes fastest.
Arguments:
- tokens: bfloat16 [8192, 2048], P(('dp', 'expert')), may hold values from -6 to 6
- cotangent: bfloat16 [8192, 2048], P(('dp', 'expert')), may hold values from -6 to 6
- expert_ids: int32 [8192, 8], P(('dp', 'expert')), may hold values from 0 to 127, all different within a row; in each aligned block of 16 rows (0 to 15, 16 to 31, ...) at most 2 rows name the same one
- gate_values: float32 [8192, 8], P(('dp', 'expert')), may hold values from 0.05 to 0.5
- gate_weight: bfloat16 [128, 2048, 384], P('expert', 'dp'), may hold values from -0.125 to 0.125
- up_weight: bfloat16 [128, 2048, 384], P('expert', 'dp'), may hold values from -0.125 to 0.125
- down_weight: bfloat16 [128, 2048, 384], P('expert', 'dp'), may hold values from -0.3125 to 0.3125
Outputs:
- mixed: bfloat16 [8192, 2048], P(('dp', 'expert'))
- input_grad: bfloat16 [8192, 2048], P(('dp', 'expert'))
- gate_grad: float32 [8192, 8], P(('dp', 'expert'))
- gate_weight_grad: float32 [128, 2048, 384], P('expert', 'dp')
- up_weight_grad: float32 [128, 2048, 384], P('expert', 'dp')
Inputs may be any that keep to these rules, and one draw needn't show every extreme that they name: `expert_ids`: each row names 8 different experts. Among the 16 rows of one device no expert is named more than 2 times.
All inputs are finite; a program needn't handle non-finite values.
Results may differ from a plain program's by a relative error of at most 0.012.
Values may be sent and summed in bfloat16 or wider, within the bound.
A program may use at most 64 MiB of HBM per device.

v0:
```python
import jax
import jax.numpy as jnp
from jax import lax
from jax.sharding import PartitionSpec as P


def body(tokens, cotangent, expert_ids, gate_values, gate_weight, up_weight, down_weight):
    tok_rows = tokens.shape[0]
    feature_width = tokens.shape[1]
    top_count = expert_ids.shape[1]
    experts = lax.axis_size("expert")
    routed = tok_rows * top_count
    capacity = min(tok_rows, max(2, (routed + experts - 1) // experts + 1))
    flat_ids = expert_ids.reshape(routed)
    onehot = (flat_ids[:, None] == jnp.arange(experts, dtype=jnp.int32)[None, :]).astype(jnp.int32)
    earlier = jnp.cumsum(onehot, axis=0) - onehot
    slot_rank = jnp.sum(earlier * onehot, axis=1)
    target = flat_ids * capacity + slot_rank
    owner_row = jnp.arange(routed, dtype=jnp.int32) // top_count
    gate_flat = gate_values.reshape(routed)
    picked = tokens[owner_row]
    scaled = (gate_flat[:, None] * cotangent[owner_row].astype(jnp.float32)).astype(jnp.bfloat16)
    slot_count = experts * capacity
    send_rows = jnp.zeros((slot_count, feature_width), jnp.bfloat16).at[target].set(picked)
    send_rows = send_rows.reshape(experts, capacity, feature_width)
    send_grads = jnp.zeros((slot_count, feature_width), jnp.bfloat16).at[target].set(scaled)
    send_grads = send_grads.reshape(experts, capacity, feature_width)
    gate_full, up_full, down_full = (
        lax.all_gather(gate_weight, "dp", axis=1, tiled=True),
        lax.all_gather(up_weight, "dp", axis=1, tiled=True),
        lax.all_gather(down_weight, "dp", axis=1, tiled=True),
    )
    gate_mat = gate_full[0]
    up_mat = up_full[0]
    arrived = lax.all_to_all(send_rows, "expert", split_axis=0, concat_axis=0, tiled=True)
    rows = arrived.reshape(slot_count, feature_width)
    hidden_gate = jnp.dot(rows, gate_mat, preferred_element_type=jnp.float32)
    hidden_up = jnp.dot(rows, up_mat, preferred_element_type=jnp.float32)
    down_mat = down_full[0]
    sigma = jax.nn.sigmoid(hidden_gate)
    active = (hidden_gate * sigma * hidden_up).astype(jnp.bfloat16)
    contract_last = (((1,), (1,)), ((), ()))
    outputs = lax.dot_general(
        active, down_mat, contract_last, preferred_element_type=jnp.float32
    ).astype(jnp.bfloat16)
    outputs = outputs.reshape(experts, capacity, feature_width)
    returned = lax.all_to_all(outputs, "expert", split_axis=0, concat_axis=0, tiled=True)
    arrived_grads = lax.all_to_all(send_grads, "expert", split_axis=0, concat_axis=0, tiled=True)
    grad_rows = arrived_grads.reshape(slot_count, feature_width)
    grad_active = jnp.dot(grad_rows, down_mat, preferred_element_type=jnp.float32)
    grad_up = (grad_active * hidden_gate * sigma).astype(jnp.bfloat16)
    grad_gate = (grad_active * hidden_up * sigma * (1.0 + hidden_gate * (1.0 - sigma))).astype(
        jnp.bfloat16
    )
    input_rows = lax.dot_general(
        grad_gate, gate_mat, contract_last, preferred_element_type=jnp.float32
    )
    input_rows = input_rows + lax.dot_general(
        grad_up, up_mat, contract_last, preferred_element_type=jnp.float32
    )
    input_rows = input_rows.astype(jnp.bfloat16).reshape(experts, capacity, feature_width)
    returned_grads = lax.all_to_all(input_rows, "expert", split_axis=0, concat_axis=0, tiled=True)
    contract_rows = (((0,), (0,)), ((), ()))
    gate_part = lax.dot_general(rows, grad_gate, contract_rows, preferred_element_type=jnp.float32)
    up_part = lax.dot_general(rows, grad_up, contract_rows, preferred_element_type=jnp.float32)
    gate_weight_grad, up_weight_grad = (
        lax.psum_scatter(
            gate_part[None].astype(jnp.bfloat16), "dp", scatter_dimension=1, tiled=True
        ).astype(jnp.float32),
        lax.psum_scatter(
            up_part[None].astype(jnp.bfloat16), "dp", scatter_dimension=1, tiled=True
        ).astype(jnp.float32),
    )
    back_rows = returned.reshape(slot_count, feature_width)[target].astype(jnp.float32)
    back_rows = back_rows.reshape(tok_rows, top_count, feature_width)
    back_grads = returned_grads.reshape(slot_count, feature_width)[target].astype(jnp.float32)
    back_grads = back_grads.reshape(tok_rows, top_count, feature_width)
    weights_here = gate_flat.reshape(tok_rows, top_count)
    mixed = jnp.sum(weights_here[:, :, None] * back_rows, axis=1).astype(jnp.bfloat16)
    gate_grad = jnp.sum(back_rows * cotangent.astype(jnp.float32)[:, None, :], axis=2)
    input_grad = jnp.sum(back_grads, axis=1).astype(jnp.bfloat16)
    return (mixed, input_grad, gate_grad, gate_weight_grad, up_weight_grad)


def solution(mesh):
    placed = (
        P(("dp", "expert"), None),
        P(("dp", "expert"), None),
        P(("dp", "expert"), None),
        P(("dp", "expert"), None),
        P("expert", "dp", None),
        P("expert", "dp", None),
        P("expert", "dp", None),
    )
    return jax.shard_map(
        body,
        mesh=mesh,
        in_specs=placed,
        out_specs=(
            P(("dp", "expert"), None),
            P(("dp", "expert"), None),
            P(("dp", "expert"), None),
            P("expert", "dp", None),
            P("expert", "dp", None),
        ),
        check_vma=False,
    )
```

profile of v0, /device:TPU:1, one launch (start us, length us, event | category | flops | bytes accessed | tf_op | source)
XLA Modules:
  0.0 289.4 jit_solution(706173469473217055)
XLA Ops:
  7.9 0.8 copy.22
  9.4 3.4 %scatter_custom_fusion = bf16[256,2048]{1,0:T(8,128)(2,1)S(1)} fusion(s32[128]{0:T(128)S(1)} %fusion.24, bf16[16,2048]{1,0:T(8,128)(2,1)S(1)} %copy-done, s32[1024]{0:T(1024)S(1)} %pad_clamp_fusion.1, bf16[]{:T(256)} %constant.26.clone.1), kind=kCustom, calls=%fused_computation.30 | custom fusion | bytes 1048578 | tf_op jit(solution)/shard_map/scatter | solution.py:24
  12.8 1.5 reshape.128
  14.3 20.7 %all-to-all-start = ((bf16[128,2,2048]{2,1,0:T(2,128)(2,1)}), bf16[128,2,2048]{2,1,0:T(2,128)(2,1)S(1)}, u32[]{:S(2)}, u32[]{:S(2)}) async-start(bf16[128,2,2048]{2,1,0:T(2,128)(2,1)} %reshape.128), calls=%async_computation | async-start | bytes 2097152 | tf_op jit(solution)/shard_map/all_to_all | solution.py:35
  36.6 3.4 %scatter_custom_fusion.1 = bf16[256,2048]{1,0:T(8,128)(2,1)S(1)} fusion(s32[128]{0:T(128)S(1)} %fusion.24, f32[128]{0:T(128)S(1)} %mul.81, bf16[]{:T(256)} %constant.26.clone.1, bf16[16,2048]{1,0:T(8,128)(2,1)S(1)} %copy-done.3, s32[1024]{0:T(1024)S(1)} %pad_clamp_fusion.1), kind=kCustom, calls=%fused_computation.28 | custom fusion | flops 786432 | bytes 1118722 | tf_op jit(solution)/shard_map/scatter | solution.py:26
  40.1 1.5 reshape.132
  41.6 45.2 %all-to-all-done = bf16[128,2,2048]{2,1,0:T(2,128)(2,1)S(1)} async-done(((bf16[128,2,2048]{2,1,0:T(2,128)(2,1)}), bf16[128,2,2048]{2,1,0:T(2,128)(2,1)S(1)}, u32[]{:S(2)}, u32[]{:S(2)}) %all-to-all-start) | async-done | bytes 1048608 | tf_op jit(solution)/shard_map/all_to_all | solution.py:35
  86.8 10.2 %all-to-all-start.2 = ((bf16[128,2,2048]{2,1,0:T(2,128)(2,1)}), bf16[128,2,2048]{2,1,0:T(2,128)(2,1)S(1)}, u32[]{:S(2)}, u32[]{:S(2)}) async-start(bf16[128,2,2048]{2,1,0:T(2,128)(2,1)} %reshape.132), calls=%async_computation.2 | async-start | bytes 2097152 | tf_op jit(solution)/shard_map/all_to_all | solution.py:48
  98.2 2.9 fusion.7
  101.1 8.3 %all-gather.4.cloned.1.call-done = bf16[1,2048,384]{2,1,0:T(8,128)(2,1)} async-done(((bf16[1,512,384]{2,1,0:T(8,128)(2,1)}), bf16[1,2048,384]{2,1,0:T(8,128)(2,1)}) %all-gather.4.cloned.1.call-update) | async-done | bytes 1572880 | tf_op jit(solution)/shard_map/all_gather | solution.py:29
  109.4 2.9 fusion.11
  112.3 33.6 %all-gather.8.cloned.1.call-done = bf16[1,2048,384]{2,1,0:T(8,128)(2,1)} async-done(((bf16[1,512,384]{2,1,0:T(8,128)(2,1)}), bf16[1,2048,384]{2,1,0:T(8,128)(2,1)}) %all-gather.8.cloned.1.call-update) | async-done | bytes 1572880 | tf_op jit(solution)/shard_map/all_gather | solution.py:31
  145.9 2.4 convolution_convert_fusion.2
  148.3 1.5 reshape.130
  149.8 17.1 %all-to-all-start.1 = ((bf16[128,2,2048]{2,1,0:T(2,128)(2,1)}), bf16[128,2,2048]{2,1,0:T(2,128)(2,1)}, u32[]{:S(2)}, u32[]{:S(2)}) async-start(bf16[128,2,2048]{2,1,0:T(2,128)(2,1)} %reshape.130), calls=%async_computation.1 | async-start | bytes 2097152 | tf_op jit(solution)/shard_map/all_to_all | solution.py:47
  167.4 2.4 multiply_convert_fusion.2
  169.8 1.9 fusion
  171.8 0.7 fusion.9
  173.2 0.8 fusion.2
  173.9 1.5 reshape.134
  175.4 43.0 %all-to-all-done.1 = bf16[128,2,2048]{2,1,0:T(2,128)(2,1)} async-done(((bf16[128,2,2048]{2,1,0:T(2,128)(2,1)}), bf16[128,2,2048]{2,1,0:T(2,128)(2,1)}, u32[]{:S(2)}, u32[]{:S(2)}) %all-to-all-start.1) | async-done | bytes 1048608 | tf_op jit(solution)/shard_map/all_to_all | solution.py:47
  218.4 10.2 %all-to-all-start.3 = ((bf16[128,2,2048]{2,1,0:T(2,128)(2,1)}), bf16[128,2,2048]{2,1,0:T(2,128)(2,1)S(1)}, u32[]{:S(2)}, u32[]{:S(2)}) async-start(bf16[128,2,2048]{2,1,0:T(2,128)(2,1)} %reshape.134), calls=%async_computation.3 | async-start | bytes 2097152 | tf_op jit(solution)/shard_map/all_to_all | solution.py:62
  228.9 1.9 fusion.1
  230.9 1.9 convert_element_type.76
  232.8 31.2 %reduce-scatter.5.cloned.1.call-done = bf16[1,512,384]{2,1,0:T(8,128)(2,1)} async-done(((bf16[1,2048,384]{2,1,0:T(8,128)(2,1)}), bf16[1,512,384]{2,1,0:T(8,128)(2,1)}) %reduce-scatter.5.cloned.1.call-update) | async-done | bytes 393232 | tf_op jit(solution)/shard_map/reduce_scatter | solution.py:70
  264.0 1.9 convert_element_type.79
  265.9 1.5 reshape.131
  267.4 0.9 gather_fusion
  268.4 1.7 fusion.14
  270.7 9.8 %all-to-all-done.3 = bf16[128,2,2048]{2,1,0:T(2,128)(2,1)S(1)} async-done(((bf16[128,2,2048]{2,1,0:T(2,128)(2,1)}), bf16[128,2,2048]{2,1,0:T(2,128)(2,1)S(1)}, u32[]{:S(2)}, u32[]{:S(2)}) %all-to-all-start.3) | async-done | bytes 1048608 | tf_op jit(solution)/shard_map/all_to_all | solution.py:62
  280.9 0.9 gather_fusion.1
  281.9 1.0 bitcast_reduce_fusion
  (41 shorter events, 6.8 us)
Async XLA Ops:
  7.2 2.2 copy-start
  14.3 22.2 %copy-start.4 = (f32[16,8]{0,1:T(8,128)S(1)}, f32[16,8]{0,1:T(8,128)}, u32[]{:S(2)}) copy-start(f32[16,8]{0,1:T(8,128)} %param.10) | copy-start | bytes 1540
  14.3 22.4 %copy-start.3 = (bf16[16,2048]{1,0:T(8,128)(2,1)S(1)}, bf16[16,2048]{1,0:T(8,128)(2,1)}, u32[]{:S(2)}) copy-start(bf16[16,2048]{1,0:T(8,128)(2,1)} %param.8) | copy-start | bytes 196612
  14.3 72.5 %all-to-all-start = ((bf16[128,2,2048]{2,1,0:T(2,128)(2,1)}), bf16[128,2,2048]{2,1,0:T(2,128)(2,1)S(1)}, u32[]{:S(2)}, u32[]{:S(2)}) async-start(bf16[128,2,2048]{2,1,0:T(2,128)(2,1)} %reshape.128), calls=%async_computation | async-start | bytes 2097152 | tf_op jit(solution)/shard_map/all_to_all | solution.py:35
  35.0 63.3 %all-gather.6.cloned.1.call-start = ((), (), s32[]{:S(2)}) async-start(), calls=%async_computation.7 | async-start | bytes 1966080 | tf_op jit(solution)/shard_map/all_gather | solution.py:30
  35.7 73.7 %all-gather.4.cloned.1.call-start = ((), (), s32[]{:S(2)}) async-start(), calls=%async_computation.6 | async-start | bytes 1966080 | tf_op jit(solution)/shard_map/all_gather | solution.py:29
  86.8 63.0 %all-to-all-start.2 = ((bf16[128,2,2048]{2,1,0:T(2,128)(2,1)}), bf16[128,2,2048]{2,1,0:T(2,128)(2,1)S(1)}, u32[]{:S(2)}, u32[]{:S(2)}) async-start(bf16[128,2,2048]{2,1,0:T(2,128)(2,1)} %reshape.132), calls=%async_computation.2 | async-start | bytes 2097152 | tf_op jit(solution)/shard_map/all_to_all | solution.py:48
  97.0 48.9 %all-gather.8.cloned.1.call-start = ((), (), s32[]{:S(2)}) async-start(), calls=%async_computation.8 | async-start | bytes 1966080 | tf_op jit(solution)/shard_map/all_gather | solution.py:31
  149.8 68.6 %all-to-all-start.1 = ((bf16[128,2,2048]{2,1,0:T(2,128)(2,1)}), bf16[128,2,2048]{2,1,0:T(2,128)(2,1)}, u32[]{:S(2)}, u32[]{:S(2)}) async-start(bf16[128,2,2048]{2,1,0:T(2,128)(2,1)} %reshape.130), calls=%async_computation.1 | async-start | bytes 2097152 | tf_op jit(solution)/shard_map/all_to_all | solution.py:47
  166.9 64.0 %reduce-scatter.3.cloned.1.call-start = ((), (), s32[]{:S(2)}) async-start(), calls=%async_computation.9 | async-start | bytes 1966080 | tf_op jit(solution)/shard_map/reduce_scatter | solution.py:67
  169.8 1.9 copy-start.2
  171.7 1.4 copy-start.1
  218.4 62.1 %all-to-all-start.3 = ((bf16[128,2,2048]{2,1,0:T(2,128)(2,1)}), bf16[128,2,2048]{2,1,0:T(2,128)(2,1)S(1)}, u32[]{:S(2)}, u32[]{:S(2)}) async-start(bf16[128,2,2048]{2,1,0:T(2,128)(2,1)} %reshape.134), calls=%async_computation.3 | async-start | bytes 2097152 | tf_op jit(solution)/shard_map/all_to_all | solution.py:62
  228.6 35.4 %reduce-scatter.5.cloned.1.call-start = ((), (), s32[]{:S(2)}) async-start(), calls=%async_computation.10 | async-start | bytes 1966080 | tf_op jit(solution)/shard_map/reduce_scatter | solution.py:70
Sparse Core Ops, SparseCore 0:
  37.9 35.0 all-gather.5
  75.1 34.3 all-gather.3
  111.5 34.3 all-gather.7
  171.9 31.9 reduce-scatter.2
  232.0 31.9 reduce-scatter.4
where the time goes:
time: 293 us; the launch traced here: 289 us
  waiting for transfers between devices  173 us (59%)
  starting transfers between devices  58.8 us (20%)
  local copies, waits for them, and re-layouts  16.5 us (6%)
  matrix products  15.8 us (5%)
  between operations  14 us (5%)
  other arithmetic  11.1 us (4%)
    all_to_all x1, waiting for transfers between devices, body(): lax.all_to_all(send_rows, 'expert', split_axis=0, concat_axis=0, tiled=True)  45.2 us
    all_to_all x1, waiting for transfers between devices, body(): lax.all_to_all(outputs, 'expert', split_axis=0, concat_axis=0, tiled=True)  43 us
    all_gather x1, waiting for transfers between devices, body(): lax.all_gather(down_weight, 'dp', axis=1, tiled=True)  33.6 us
    reduce_scatter x1, waiting for transfers between devices, body(): lax.psum_scatter(up_part[None].astype(jnp.bfloat16), 'dp', scatter_dimens...  31.2 us
    all_to_all x1, starting transfers between devices, body(): lax.all_to_all(send_rows, 'expert', split_axis=0, concat_axis=0, tiled=True)  20.7 us
    all_to_all x1, starting transfers between devices, body(): lax.all_to_all(outputs, 'expert', split_axis=0, concat_axis=0, tiled=True)  17.1 us
    all_to_all x1, starting transfers between devices, body(): lax.all_to_all(input_rows, 'expert', split_axis=0, concat_axis=0, tiled=T...  10.2 us
    all_to_all x1, starting transfers between devices, body(): lax.all_to_all(send_grads, 'expert', split_axis=0, concat_axis=0, tiled=T...  10.2 us
  transfers between devices with their start and end apart: 9, of which 6 were waited for; matrix products, arithmetic and copies ran while one was open for 12% of the time, Pallas kernels for 0%

commit v1 on v0

v1 whole, which is shorter than its diff:
```python
import functools

import jax
import jax.numpy as jnp
from jax import lax
from jax.experimental import pallas as pl
from jax.experimental.pallas import tpu as pltpu
from jax.sharding import PartitionSpec as P

MESH = pl.DeviceIdType.MESH
NX, NZ, NJ = 4, 16, 8
TOK, D, H, TOP = 16, 2048, 384, 8
NB = 8
ROWS = NB * TOK
COLS = 512
F32, BF16 = jnp.float32, jnp.bfloat16
NT = (((1,), (1,)), ((), ()))


def dot(a, b):
    return jnp.dot(a, b, preferred_element_type=F32)


def dot_t(a, b):
    return lax.dot_general(a, b, NT, preferred_element_type=F32)


def iota(shape, dim):
    return lax.broadcasted_iota(jnp.int32, shape, dim)


def halves(v):
    hi = v.astype(BF16)
    return hi, (v - hi.astype(F32)).astype(BF16)


def kernel(
    tok_ref, cot_ref, meta_ref, gw_ref, uw_ref, dw_ref,
    mixed_ref, igrad_ref, gg_ref, ggw_ref, guw_ref,
    W, AG, MT, STG, ROW, PCOT, XT, HG, HU, ACT, DGU, OST, RET, PART, RSS, RSR, PS, PR, GGS, GGR, ONE, TG, EX,
    w_s, w_r, l_s, ag_s, ag_r, mt_s, mt_r, di_s, di_r, re_s, re_r, rs_s, rs_r, p_s, p_r, gg_s, gg_r,
):
    x = lax.axis_index("dp")
    e = lax.axis_index("expert")
    z = e // NJ
    j = lax.rem(e, NJ)

    def zpeer(d):
        return {"dp": x, "expert": lax.rem(z + d + NZ, NZ) * NJ + j}

    def jat(q):
        return lax.rem(j + q + NJ, NJ)

    def xat(q):
        return lax.rem(x + q + NX, NX)

    def jpeer(q):
        return {"dp": x, "expert": z * NJ + jat(q)}

    def xpeer(q):
        return {"dp": xat(q), "expert": e}

    barrier = pltpu.get_barrier_semaphore()
    peers = [zpeer(d) for d in range(1, NZ)] + [jpeer(q) for q in range(1, NJ)] + [xpeer(q) for q in range(1, NX)]
    for peer in peers:
        pl.semaphore_signal(barrier, inc=1, device_id=peer, device_id_type=MESH)
    pl.semaphore_wait(barrier, len(peers))

    sent = []

    def send(src, dst, s, r, peer):
        copy = pltpu.make_async_remote_copy(
            src_ref=src, dst_ref=dst, send_sem=s, recv_sem=r, device_id=peer, device_id_type=MESH
        )
        copy.start()
        sent.append(copy)
        return copy

    arrive = {}

    def ag_send(tc, r, step):
        to = (r - step) % NZ
        src = (tok_ref, cot_ref)[tc] if r == 4 else AG.at[tc, r]
        arrive[tc, to] = send(src, AG.at[tc, to], ag_s.at[tc, to], ag_r.at[tc, to], zpeer(step))

    for tc in (0, 1):
        ag_send(tc, 4, 8)
        ag_send(tc, 4, 1)
        ag_send(tc, 4, -1)
        if tc == 0:
            meta = [
                send(meta_ref, MT.at[(4 - d) % NZ], mt_s.at[d], mt_r.at[d], zpeer(d)) for d in range(1, NZ)
            ]
    own = []
    weights = {}
    for i, ref in enumerate((gw_ref, uw_ref, dw_ref)):
        for q in (2, 1, 3):
            weights[i, q] = send(ref.at[0], W.at[i, x], w_s.at[i, q], w_r.at[i, q], xpeer(q))
        copy = pltpu.make_async_copy(ref.at[0], W.at[i, x], l_s.at[i])
        copy.start()
        own.append(copy)
    MT[4] = meta_ref[...]
    AG[0, 4] = tok_ref[...]
    AG[1, 4] = cot_ref[...]

    def hop(base, h):
        for tc in (0, 1):
            if h == 0:
                if base == 12:
                    arrive[tc, 12].wait_recv()
                    ag_send(tc, 12, 1)
                    ag_send(tc, 12, -1)
                continue
            arrive[tc, base - h].wait_recv()
            if h < 4:
                ag_send(tc, base - h, 1)
                arrive[tc, base + h].wait_recv()
                if h < 3:
                    ag_send(tc, base + h, -1)

    def select(ch):
        m = MT[pl.ds(NB * ch, NB)].reshape(NB * 8, 128).astype(BF16)
        row, col = iota((ROWS, NB * 8), 0), iota((ROWS, NB * 8), 1)
        mine = lax.rem(row, 16) // 2 * 8
        codes = dot((col == mine).astype(F32).astype(BF16), m)
        gates = dot(((col == mine + 1) | (col == mine + 2)).astype(F32).astype(BF16), m)
        row = iota((ROWS, 128), 0)
        col = iota((ROWS, 128), 1)
        want = ((z * NJ + row // 16) * 2 + lax.rem(row, 2)).astype(F32)
        taken = (codes == want).astype(F32)
        gate = jnp.sum(taken * gates, axis=1, keepdims=True)
        fold = (row // TOP == lax.rem(col, TOK)).astype(F32).astype(BF16)
        one = dot(taken.astype(BF16), fold)
        one = jnp.where(lax.rem(row, 16) // 2 == col // TOK, one, 0.0)
        EX[ch] = taken.astype(BF16)
        ONE[ch] = one.astype(BF16)
        one_t = one.T
        TG[ch, 0] = one_t.astype(BF16)
        gated = (one * gate).T
        hi, lo = halves(gated)
        TG[ch, 1] = hi
        TG[ch, 2] = lo
        return gate

    rows_in = {}

    def pack(ch, gate):
        one = ONE[ch]

        @pl.loop(0, D // COLS)
        def _(n):
            at = pl.ds(pl.multiple_of(n * COLS, COLS), COLS)
            block = AG[0, pl.ds(NB * ch, NB), :, at].reshape(ROWS, COLS)
            STG[ch, 0, :, :, at] = dot(one, block).astype(BF16).reshape(NJ, 16, COLS)
            block = AG[1, pl.ds(NB * ch, NB), :, at].reshape(ROWS, COLS)
            picked = dot(one, block)
            PCOT[ch, :, at] = picked.astype(BF16)
            STG[ch, 1, :, :, at] = (picked * gate).astype(BF16).reshape(NJ, 16, COLS)

        for tc in (0, 1):
            for q in range(1, NJ):
                rows_in[ch, tc, q] = send(
                    STG.at[ch, tc, jat(q)], ROW.at[tc, ch, j], di_s.at[ch, tc, q], di_r.at[ch, tc, q], jpeer(q)
                )
            ROW[tc, ch, j] = STG[ch, tc, j]

    hop(4, 1)
    hop(12, 0)
    hop(4, 2)
    for copy in meta:
        copy.wait_recv()
    gate_a = select(0)
    hop(12, 1)
    hop(4, 3)
    gate_b = select(1)
    hop(12, 2)
    hop(4, 4)
    hop(12, 3)
    pack(0, gate_a)
    hop(12, 4)
    pack(1, gate_b)
    for ch in (0, 1):
        for tc in (0, 1):
            for q in range(1, NJ):
                rows_in[ch, tc, q].wait_recv()

    @pl.loop(0, D // COLS)
    def _(n):
        at = pl.ds(pl.multiple_of(n * COLS, COLS), COLS)
        XT[at, :] = ROW[0, :, :, :, at].reshape(2 * ROWS, COLS).T

    def weight_in(i):
        own[i].wait()
        for q in range(1, NX):
            weights[i, q].wait_recv()

    def rows_by(i, tc, to):
        to[...] = jnp.zeros_like(to)

        @pl.loop(0, NX)
        def _(n):
            at = pl.ds(pl.multiple_of(n * COLS, COLS), COLS)
            to[...] += dot(ROW[tc, :, :, :, at].reshape(2 * ROWS, COLS), W[i, n])

    weight_in(0)
    rows_by(0, 0, HG)
    weight_in(1)
    rows_by(1, 0, HU)
    hg, hu = HG[...], HU[...]
    sigma = jax.nn.sigmoid(hg)
    ACT[...] = (hg * sigma * hu).astype(BF16)
    weight_in(2)

    back = {}

    def give_back(arr):
        for ch in (1, 0):
            for q in range(1, NJ):
                back[arr, ch, q] = send(
                    OST.at[arr, ch, jat(q)], RET.at[arr, ch, j], re_s.at[arr, ch, q], re_r.at[arr, ch, q], jpeer(q)
                )
            RET[arr, ch, j] = OST[arr, ch, j]

    @pl.loop(0, NX)
    def _(n):
        at = pl.ds(pl.multiple_of(n * COLS, COLS), COLS)
        OST[0, :, :, :, at] = dot_t(ACT[...], W[2, n]).astype(BF16).reshape(2, NJ, 16, COLS)

    give_back(0)
    rows_by(2, 1, HU)
    da = HU[...]
    DGU[1] = (da * hg * sigma).astype(BF16)
    DGU[0] = (da * hu * sigma * (1.0 + hg * (1.0 - sigma))).astype(BF16)

    @pl.loop(0, NX)
    def _(n):
        at = pl.ds(pl.multiple_of(n * COLS, COLS), COLS)
        dx = dot_t(DGU[0], W[0, n]) + dot_t(DGU[1], W[1, n])
        OST[1, :, :, :, at] = dx.astype(BF16).reshape(2, NJ, 16, COLS)

    give_back(1)

    @pl.loop(0, NX)
    def _(n):
        at = pl.ds(pl.multiple_of(n * COLS, COLS), COLS)
        PS[0, n] = dot(XT[at, :], DGU[0]).astype(BF16)
        PS[1, n] = dot(XT[at, :], DGU[1]).astype(BF16)

    parts = [
        send(PS.at[arr, xat(q)], PR.at[arr, q], p_s.at[arr, q], p_r.at[arr, q], xpeer(q))
        for arr in (0, 1)
        for q in (2, 1, 3)
    ]

    def combine(arr, ch):
        for q in range(1, NJ):
            back[arr, ch, q].wait_recv()

        def step(n, dots):
            at = pl.ds(pl.multiple_of(n * COLS, COLS), COLS)
            block = RET[arr, ch, :, :, at].reshape(ROWS, COLS)
            if arr == 0:
                part = dot(TG[ch, 1], block) + dot(TG[ch, 2], block)
                dots = dots + jnp.sum(block.astype(F32) * PCOT[ch, :, at].astype(F32), axis=1, keepdims=True)
            else:
                part = dot(TG[ch, 0], block)
            PART[arr, pl.ds(NB * ch, NB), :, at] = part.reshape(NB, TOK, COLS)
            return dots

        return lax.fori_loop(0, D // COLS, step, jnp.zeros((ROWS, 1), F32))

    arrived = {}

    def rs_send(arr, r, step, to, value):
        RSS[arr, r] = value.astype(BF16)
        arrived[arr, to] = send(RSS.at[arr, r], RSR.at[arr, to], rs_s.at[arr, to], rs_r.at[arr, to], zpeer(step))

    def rs_take(arr, r):
        arrived[arr, r].wait_recv()
        return RSR[arr, r].astype(F32)

    def rs_start(arr, base):
        rs_send(arr, base - 4, -1, base - 3, PART[arr, base - 4])
        rs_send(arr, base + 3, 1, base + 2, PART[arr, base + 3])

    def rs_hop(arr, base, h):
        r = base - 4 + h
        rs_send(arr, r, -1, r + 1, PART[arr, r] + rs_take(arr, r))
        if h < 3:
            r = base + 3 - h
            to = r - 1 if h < 2 else base + 3
            rs_send(arr, r, 1, to, PART[arr, r] + rs_take(arr, r))

    def rs_sum(arr, base):
        return PART[arr, base] + rs_take(arr, base) + rs_take(arr, base + 3)

    gg = {}

    def gates_back(ch, dots):
        taken = EX[ch].astype(F32)
        row, col = iota((NB * 8, ROWS), 0), iota((NB * 8, ROWS), 1)
        pick = (row == lax.rem(col, 16) // 2 * 8).astype(F32).astype(BF16)
        hi, lo = halves(taken * dots)
        GGS[pl.ds(NB * ch, NB)] = (dot(pick, hi) + dot(pick, lo)).reshape(NB, 8, 128)
        for r in range(NB * ch, NB * ch + NB):
            if r != 4:
                d = (r - 4) % NZ
                gg[d] = send(GGS.at[r], GGR.at[d], gg_s.at[d], gg_r.at[d], zpeer(d))

    for arr in (0, 1):
        for ch in (1, 0):
            dots = combine(arr, ch)
            rs_start(arr, 4 + NB * ch)
            if arr == 0:
                gates_back(ch, dots)
    for h in (1, 2, 3):
        for base in (12, 4):
            for arr in (0, 1):
                rs_hop(arr, base, h)
    for arr in (0, 1):
        rs_send(arr, 12, 8, 0, rs_sum(arr, 12))
    for copy in parts:
        copy.wait_recv()
    for arr, ref in ((0, ggw_ref), (1, guw_ref)):
        total = PS[arr, x].astype(F32)
        for q in range(1, NX):
            total = total + PR[arr, q].astype(F32)
        ref[0] = total
    total = GGS[4]
    for d in range(1, NZ):
        gg[d].wait_recv()
        total = total + GGR[d]
    gg_ref[...] = total
    for arr, ref in ((0, mixed_ref), (1, igrad_ref)):
        ref[...] = (rs_sum(arr, 4) + rs_take(arr, 0)).astype(BF16)
    for copy in sent:
        copy.wait_send()


def body(tokens, cotangent, expert_ids, gate_values, gate_weight, up_weight, down_weight):
    flat = expert_ids.reshape(1, TOK * TOP)
    route = jnp.arange(TOK * TOP)
    same = (flat.reshape(TOK * TOP, 1) == flat) & (route[:, None] < route[None, :])
    rank = jnp.sum(same.astype(jnp.int32), axis=0, keepdims=True)
    code = (flat * 2 + rank).astype(F32)
    gates = gate_values.reshape(1, TOK * TOP)
    hi = lax.reduce_precision(gates, 8, 7)
    meta = jnp.concatenate([code, hi, gates - hi, jnp.zeros((5, TOK * TOP), F32)], axis=0)

    vmem = pl.BlockSpec(memory_space=pltpu.VMEM)
    hbm = pl.BlockSpec(memory_space=pl.ANY)
    dma = pltpu.SemaphoreType.DMA
    v = pltpu.VMEM
    outs = (
        jax.ShapeDtypeStruct((TOK, D), BF16),
        jax.ShapeDtypeStruct((TOK, D), BF16),
        jax.ShapeDtypeStruct((8, 128), F32),
        jax.ShapeDtypeStruct((1, COLS, H), F32),
        jax.ShapeDtypeStruct((1, COLS, H), F32),
    )
    mixed, igrad, gg, ggw, guw = pl.pallas_call(
        kernel,
        out_shape=outs,
        in_specs=[vmem] * 3 + [hbm] * 3,
        out_specs=[vmem] * 5,
        scratch_shapes=[
            v((3, NX, COLS, H), BF16),
            v((2, NZ, TOK, D), BF16),
            v((NZ, 8, 128), F32),
            v((2, 2, NJ, 16, D), BF16),
            v((2, 2, NJ, 16, D), BF16),
            v((2, ROWS, D), BF16),
            v((D, 2 * ROWS), BF16),
            v((2 * ROWS, H), F32),
            v((2 * ROWS, H), F32),
            v((2 * ROWS, H), BF16),
            v((2, 2 * ROWS, H), BF16),
            v((2, 2, NJ, 16, D), BF16),
            v((2, 2, NJ, 16, D), BF16),
            v((2, NZ, TOK, D), F32),
            v((2, NZ, TOK, D), BF16),
            v((2, NZ, TOK, D), BF16),
            v((2, NX, COLS, H), BF16),
            v((2, NX, COLS, H), BF16),
            v((NZ, 8, 128), F32),
            v((NZ, 8, 128), F32),
            v((2, ROWS, ROWS), BF16),
            v((2, 3, ROWS, ROWS), BF16),
            v((2, ROWS, 128), BF16),
            dma((3, NX)), dma((3, NX)), dma((3,)),
            dma((2, NZ)), dma((2, NZ)),
            dma((NZ,)), dma((NZ,)),
            dma((2, 2, NJ)), dma((2, 2, NJ)),
            dma((2, 2, NJ)), dma((2, 2, NJ)),
            dma((2, NZ)), dma((2, NZ)),
            dma((2, NX)), dma((2, NX)),
            dma((NZ,)), dma((NZ,)),
        ],
        compiler_params=pltpu.CompilerParams(
            collective_id=0, has_side_effects=True, vmem_limit_bytes=48 * 2**20
        ),
        name="experts",
    )(tokens, cotangent, meta, gate_weight, up_weight, down_weight)
    return mixed, igrad, gg[0].reshape(TOK, TOP), ggw, guw


def solution(mesh):
    token = P(("dp", "expert"), None)
    weight = P("expert", "dp", None)
    return jax.shard_map(
        body,
        mesh=mesh,
        in_specs=(token,) * 4 + (weight,) * 3,
        out_specs=(token,) * 3 + (weight,) * 2,
        check_vma=False,
    )
```

time: 293 us -> 155 us (0.53); the launches traced: 289 us -> 155 us
  waiting for transfers between devices: 173 us -> 0 us
  Pallas kernels: 0 us -> 144 us
  starting transfers between devices: 58.8 us -> 0 us
  matrix products: 15.8 us -> 0 us
  between operations: 14 us -> 0.68 us
  other arithmetic: 11.1 us -> 0.88 us
  local copies, waits for them, and re-layouts: 16.5 us -> 9.56 us
    pallas_call x0 -> x1, Pallas kernels: none -> 144 us  [body(): pl.pallas_call(kernel, out_shape=outs, in_specs=[vmem] * 3 + [hbm] * 3, o...]
    all_to_all x4 -> x0, waiting for transfers between devices: 98 us -> none  [the longest x1 45.2 us: body(): lax.all_to_all(send_rows, 'expert', split_axis=0, concat_axis=0, tiled=True)]
    all_to_all x4 -> x0, starting transfers between devices: 58.2 us -> none  [the longest x1 20.7 us: body(): lax.all_to_all(send_rows, 'expert', split_axis=0, concat_axis=0, tiled=True)]
    all_gather x3 -> x0, waiting for transfers between devices: 41.9 us -> none  [the longest x1 33.6 us: body(): lax.all_gather(down_weight, 'dp', axis=1, tiled=True)]
    reduce_scatter x2 -> x0, waiting for transfers between devices: 31.2 us -> none  [the longest x1 31.2 us: body(): lax.psum_scatter(up_part[None].astype(jnp.bfloat16), 'dp', scatter_dimens...]
    dot_general x8 -> x0, matrix products: 15.8 us -> none  [the longest x1 2.87 us: body(): hidden_up = jnp.dot(rows, up_mat, preferred_element_type=jnp.float32)]
    reshape x8 -> x1, local copies, waits for them, and re-layouts: 8.79 us -> 0.09 us  [body(): gates = gate_values.reshape(1, TOK * TOP)]
    unnamed x13 -> x17, local copies, waits for them, and re-layouts: 2.17 us -> 9.04 us
  transfers between devices with their start and end apart: 9 -> 0, of which waited for: 6 -> 0; matrix products, arithmetic and copies ran while one was open for 12% -> 0% of each run, Pallas kernels for 0% -> 0%
where the time goes in v1:
time: 155 us
  Pallas kernels  144 us (93%)
  local copies, waits for them, and re-layouts  9.56 us (6%)
    pallas_call x1, Pallas kernels, body(): pl.pallas_call(kernel, out_shape=outs, in_specs=[vmem] * 3 + [hbm] * 3, o...  144 us
    unnamed x17, local copies, waits for them, and re-layouts  9.04 us

profile of v1, /device:TPU:1, one launch (start us, length us, event | category | flops | bytes accessed | tf_op | source)
XLA Modules:
  0.0 154.8 jit_solution(2429991640258168079)
XLA Ops:
  0.6 0.0 copy-start.3
  0.7 0.1 pad.3.clone
  0.7 0.7 broadcast_multiply_fusion
  1.4 0.1 copy.20
  1.5 0.1 mul.19
  1.6 0.8 copy.22
  2.3 0.1 reshape.70
  2.4 0.8 copy.21
  3.2 0.1 eq.15
  3.3 0.1 convert_reduce_fusion
  3.4 0.1 maximum_maximum_fusion.meta_ref
  3.5 0.0 copy-done.3
  3.5 0.0 copy-start
  3.5 1.0 copy-done
  4.5 0.0 copy-start.1
  4.5 1.0 copy-done.1
  5.5 0.0 copy-start.2
  5.5 1.0 copy-done.2
  6.5 0.0 copy-start.4
  6.5 0.8 copy-done.4
  7.3 143.7 %experts.1 = (bf16[16,2048]{1,0:T(8,128)(2,1)S(1)}, bf16[16,2048]{1,0:T(8,128)(2,1)S(1)}, f32[8,128]{1,0:T(8,128)S(1)}, f32[1,512,384]{2,1,0:T(8,128)S(1)}, f32[1,512,384]{2,1,0:T(8,128)S(1)}) custom-call(bf16[16,2048]{1,0:T(8,128)(2,1)S(1)} %copy-done.3, bf16[16,2048]{1,0:T(8,128)(2,1)S(1)} %copy-done.4, f32[8,128]{1,0:T(8,128)S(1)} %maximum_maximum_fusion.meta_ref, ...), custom_call_target="tpu_custom_call" | custom-call | tf_op jit(solution)/shard_map/experts/pallas_call | solution.py:361
  151.0 0.1 reshape_squeeze.3
  151.1 0.7 copy.23
  151.8 0.6 copy.28
  152.4 0.6 copy.29
  153.0 0.9 copy.30
  153.9 0.9 copy.31
  (4 shorter events, 0.0 us)
Async XLA Ops:
  0.6 2.8 %copy-start.3 = (bf16[16,2048]{1,0:T(8,128)(2,1)S(1)}, bf16[16,2048]{1,0:T(8,128)(2,1)}, u32[]{:S(2)}) copy-start(bf16[16,2048]{1,0:T(8,128)(2,1)} %tok_ref.1) | copy-start | bytes 196612
  3.5 1.0 copy-start
  4.5 1.0 copy-start.1
  5.5 1.0 copy-start.2
  6.5 0.8 copy-start.4

commit v2 on v1

v2 whole, which is shorter than its diff:
```python
import functools

import jax
import jax.numpy as jnp
from jax import lax
from jax.experimental import pallas as pl
from jax.experimental.pallas import tpu as pltpu
from jax.sharding import PartitionSpec as P

MESH = pl.DeviceIdType.MESH
NX, NZ, NJ = 4, 16, 8
TOK, D, H, TOP = 16, 2048, 384, 8
NB = 8
ROWS = NB * TOK
COLS = 512
WIDE = D + 128
F32, BF16 = jnp.float32, jnp.bfloat16
NT = (((1,), (1,)), ((), ()))


def dot(a, b):
    return jnp.dot(a, b, preferred_element_type=F32)


def dot_t(a, b):
    return lax.dot_general(a, b, NT, preferred_element_type=F32)


def iota(shape, dim):
    return lax.broadcasted_iota(jnp.int32, shape, dim)


def halves(v):
    hi = v.astype(BF16)
    return hi, (v - hi.astype(F32)).astype(BF16)


def kernel(
    tok_ref, cot_ref, meta_ref, gw_ref, uw_ref, dw_ref,
    mixed_ref, igrad_ref, gg_ref, ggw_ref, guw_ref,
    W, AGT, AGC, STG, ROW, PCOT, XT, HG, HU, ACT, DGU, OST, RET, PARTM, PARTX, RSSM, RSSX, RSRM, RSRX, PS, PR, ONE, TG, EX,
    w_s, w_r, l_s, ag_s, ag_r, di_s, di_r, re_s, re_r, rs_s, rs_r, p_s, p_r,
):
    x = lax.axis_index("dp")
    e = lax.axis_index("expert")
    z = e // NJ
    j = lax.rem(e, NJ)

    def zpeer(d):
        return {"dp": x, "expert": lax.rem(z + d + NZ, NZ) * NJ + j}

    def jat(q):
        return lax.rem(j + q + NJ, NJ)

    def xat(q):
        return lax.rem(x + q + NX, NX)

    def jpeer(q):
        return {"dp": x, "expert": z * NJ + jat(q)}

    def xpeer(q):
        return {"dp": xat(q), "expert": e}

    barrier = pltpu.get_barrier_semaphore()
    peers = [zpeer(d) for d in (1, -1, 2, -2)] + [jpeer(q) for q in range(1, NJ)] + [xpeer(q) for q in range(1, NX)]
    for peer in peers:
        pl.semaphore_signal(barrier, inc=1, device_id=peer, device_id_type=MESH)
    pl.semaphore_wait(barrier, len(peers))

    sent = []

    def send(src, dst, s, r, peer):
        copy = pltpu.make_async_remote_copy(
            src_ref=src, dst_ref=dst, send_sem=s, recv_sem=r, device_id=peer, device_id_type=MESH
        )
        copy.start()
        sent.append(copy)
        return copy

    AG = (AGT, AGC)
    arrive = {}

    def ag_send(tc, r, *steps):
        for step in steps:
            to = (r - step) % NZ
            arrive[tc, to] = send(AG[tc].at[r], AG[tc].at[to], ag_s.at[tc, to], ag_r.at[tc, to], zpeer(step))

    def ag_stage(tc, stage):
        if stage == 0:
            ag_send(tc, 4, 2, -2, 1, -1)
            return
        r = 4 - 2 * stage
        arrive[tc, r % NZ].wait_recv()
        ag_send(tc, r % NZ, 2, 1)
        r = 4 + 2 * stage
        arrive[tc, r].wait_recv()
        ag_send(tc, r, *((-2, -1) if stage < 3 else (-1,)))

    def ag_wait(tc, *places):
        for r in places:
            arrive[tc, r].wait_recv()

    AGT[4, :, :D] = tok_ref[...]
    AGT[4, :, D:] = meta_ref[...]
    AGC[4] = cot_ref[...]
    ag_stage(0, 0)

    HALF = COLS // 2
    own = []
    weights = {}
    relays = {}
    for i, ref in enumerate((gw_ref, uw_ref, dw_ref)):
        for q in (1, 3):
            weights[i, q] = send(ref.at[0], W.at[i, x], w_s.at[i, q], w_r.at[i, q], xpeer(q))
        copy = pltpu.make_async_copy(ref.at[0], W.at[i, x], l_s.at[i])
        copy.start()
        own.append(copy)

    def relay(i):
        for q, half in ((1, 0), (3, 1)):
            weights[i, q].wait_recv()
            block = W.at[i, xat(-q), pl.ds(half * HALF, HALF)]
            relays[i, half] = send(block, block, w_s.at[i, 2 * half], w_r.at[i, 2 * half], xpeer(q))

    def select(ch):
        m = AGT[pl.ds(NB * ch, NB), :, D:].reshape(ROWS, 128)
        row, col = iota((ROWS, ROWS), 0), iota((ROWS, ROWS), 1)
        mine = lax.rem(row, 16) // 2 * TOK
        codes = dot((col == mine).astype(F32).astype(BF16), m)
        gates = dot(((col == mine + 1) | (col == mine + 2)).astype(F32).astype(BF16), m)
        row = iota((ROWS, 128), 0)
        col = iota((ROWS, 128), 1)
        want = ((z * NJ + row // 16) * 2 + lax.rem(row, 2)).astype(F32)
        taken = (codes == want).astype(F32)
        gate = jnp.sum(taken * gates, axis=1, keepdims=True)
        fold = (row // TOP == lax.rem(col, TOK)).astype(F32).astype(BF16)
        one = dot(taken.astype(BF16), fold)
        one = jnp.where(lax.rem(row, 16) // 2 == col // TOK, one, 0.0)
        EX[ch] = taken.astype(BF16)
        ONE[ch] = one.astype(BF16)
        one_t = one.T
        TG[ch, 0] = one_t.astype(BF16)
        gated = (one * gate).T
        hi, lo = halves(gated)
        TG[ch, 1] = hi
        TG[ch, 2] = lo
        return gate

    rows_in = {}

    def pack(tc, ch, gate):
        one = ONE[ch]

        @pl.loop(0, D // COLS)
        def _(n):
            at = pl.ds(pl.multiple_of(n * COLS, COLS), COLS)
            picked = dot(one, AG[tc][pl.ds(NB * ch, NB), :, at].reshape(ROWS, COLS))
            if tc == 1:
                PCOT[ch, :, at] = picked.astype(BF16)
                picked = picked * gate
            STG[ch, tc, :, :, at] = picked.astype(BF16).reshape(NJ, 16, COLS)

        for q in range(1, NJ):
            rows_in[ch, tc, q] = send(
                STG.at[ch, tc, jat(q)], ROW.at[tc, ch, j], di_s.at[ch, tc, q], di_r.at[ch, tc, q], jpeer(q)
            )
        ROW[tc, ch, j] = STG[ch, tc, j]

    def rows_wait(tc):
        for ch in (0, 1):
            for q in range(1, NJ):
                rows_in[ch, tc, q].wait_recv()

    ag_stage(0, 1)
    ag_stage(1, 0)
    ag_stage(0, 2)
    ag_stage(1, 1)
    ag_wait(0, 1, 3, 5, 7)
    gate_a = select(0)
    ag_stage(0, 3)
    ag_stage(1, 2)
    pack(0, 0, gate_a)
    relay(0)
    ag_wait(0, 9, 11, 12, 13, 15)
    gate_b = select(1)
    ag_stage(1, 3)
    pack(0, 1, gate_b)
    relay(1)
    ag_wait(1, 1, 3, 5, 7)
    pack(1, 0, gate_a)
    relay(2)
    ag_wait(1, 9, 11, 12, 13, 15)
    pack(1, 1, gate_b)
    rows_wait(0)

    @pl.loop(0, D // COLS)
    def _(n):
        at = pl.ds(pl.multiple_of(n * COLS, COLS), COLS)
        XT[at, :] = ROW[0, :, :, :, at].reshape(2 * ROWS, COLS).T

    def weight_in(i):
        own[i].wait()
        for half in (0, 1):
            relays[i, half].wait_recv()

    def rows_by(i, tc, to):
        to[...] = jnp.zeros_like(to)

        @pl.loop(0, NX)
        def _(n):
            at = pl.ds(pl.multiple_of(n * COLS, COLS), COLS)
            to[...] += dot(ROW[tc, :, :, :, at].reshape(2 * ROWS, COLS), W[i, n])

    weight_in(0)
    rows_by(0, 0, HG)
    weight_in(1)
    rows_by(1, 0, HU)
    hg, hu = HG[...], HU[...]
    sigma = jax.nn.sigmoid(hg)
    ACT[...] = (hg * sigma * hu).astype(BF16)
    weight_in(2)

    back = {}

    def give_back(arr):
        for ch in (1, 0):
            for q in range(1, NJ):
                back[arr, ch, q] = send(
                    OST.at[arr, ch, jat(q)], RET.at[arr, ch, j], re_s.at[arr, ch, q], re_r.at[arr, ch, q], jpeer(q)
                )
            RET[arr, ch, j] = OST[arr, ch, j]

    @pl.loop(0, NX)
    def _(n):
        at = pl.ds(pl.multiple_of(n * COLS, COLS), COLS)
        OST[0, :, :, :, at] = dot_t(ACT[...], W[2, n]).astype(BF16).reshape(2, NJ, 16, COLS)

    give_back(0)
    rows_wait(1)
    rows_by(2, 1, HU)
    da = HU[...]
    DGU[1] = (da * hg * sigma).astype(BF16)
    DGU[0] = (da * hu * sigma * (1.0 + hg * (1.0 - sigma))).astype(BF16)

    @pl.loop(0, NX)
    def _(n):
        at = pl.ds(pl.multiple_of(n * COLS, COLS), COLS)
        PS[0, n] = dot(XT[at, :], DGU[0]).astype(BF16)
        PS[1, n] = dot(XT[at, :], DGU[1]).astype(BF16)

    parts = [
        send(PS.at[arr, xat(q)], PR.at[arr, q], p_s.at[arr, q], p_r.at[arr, q], xpeer(q))
        for arr in (0, 1)
        for q in (2, 1, 3)
    ]

    @pl.loop(0, NX)
    def _(n):
        at = pl.ds(pl.multiple_of(n * COLS, COLS), COLS)
        dx = dot_t(DGU[0], W[0, n]) + dot_t(DGU[1], W[1, n])
        OST[1, :, :, :, at] = dx.astype(BF16).reshape(2, NJ, 16, COLS)

    give_back(1)

    PART, RSS, RSR = (PARTM, PARTX), (RSSM, RSSX), (RSRM, RSRX)

    def combine(arr, ch):
        for q in range(1, NJ):
            back[arr, ch, q].wait_recv()

        def step(n, dots):
            at = pl.ds(pl.multiple_of(n * COLS, COLS), COLS)
            block = RET[arr, ch, :, :, at].reshape(ROWS, COLS)
            if arr == 0:
                part = dot(TG[ch, 1], block) + dot(TG[ch, 2], block)
                dots = dots + jnp.sum(block.astype(F32) * PCOT[ch, :, at].astype(F32), axis=1, keepdims=True)
            else:
                part = dot(TG[ch, 0], block)
            PART[arr][pl.ds(NB * ch, NB), :, at] = part.reshape(NB, TOK, COLS)
            return dots

        dots = lax.fori_loop(0, D // COLS, step, jnp.zeros((ROWS, 1), F32))
        if arr == 0:
            hi, lo = halves(EX[ch].astype(F32) * dots)
            row, col = iota((ROWS, ROWS), 0), iota((ROWS, ROWS), 1)
            first = lax.rem(col, 16) // 2 * TOK
            grads = dot((row == first).astype(F32).astype(BF16), hi) + dot((row == first + 1).astype(F32).astype(BF16), lo)
            PARTM[pl.ds(NB * ch, NB), :, D:] = grads.reshape(NB, TOK, 128)

    arrived = {}

    def rs_send(arr, r, step):
        value = rs_sum(arr, r)
        RSS[arr][r] = value.astype(BF16)
        arrived[arr, r] = send(RSS[arr].at[r], RSR[arr].at[r], rs_s.at[arr, r], rs_r.at[arr, r], zpeer(step))

    takes = {14: (12, 13), 10: (11,), 0: (14, 15), 8: (10, 9), 2: (0, 1), 6: (8, 7), 4: (2, 6, 3, 5)}

    def rs_sum(arr, r):
        value = PART[arr][r]
        for other in takes.get(r, ()):
            arrived[arr, other].wait_recv()
            value = value + RSR[arr][other].astype(F32)
        return value

    def leaves(arr, ch):
        combine(arr, ch)
        for r, step in ((12, -2), (11, 1), (13, -1), (15, -1), (9, 1)) if ch else ((1, -1), (7, 1), (3, -1), (5, 1)):
            rs_send(arr, r, step)

    def inner(arr, stage):
        r = (14, 0, 2)[stage]
        rs_send(arr, r, -2)
        r = (10, 8, 6)[stage]
        rs_send(arr, r, 2)

    leaves(0, 1)
    leaves(0, 0)
    inner(0, 0)
    leaves(1, 1)
    inner(0, 1)
    leaves(1, 0)
    inner(1, 0)
    inner(0, 2)
    inner(1, 1)
    total = rs_sum(0, 4)
    mixed_ref[...] = total[:, :D].astype(BF16)
    gg_ref[...] = jnp.broadcast_to(total[0:1, D:] + total[1:2, D:], (8, 128))
    inner(1, 2)
    for copy in parts:
        copy.wait_recv()
    for arr, ref in ((0, ggw_ref), (1, guw_ref)):
        total = PS[arr, x].astype(F32)
        for q in range(1, NX):
            total = total + PR[arr, q].astype(F32)
        ref[0] = total
    igrad_ref[...] = rs_sum(1, 4).astype(BF16)
    for copy in sent:
        copy.wait_send()


def body(tokens, cotangent, expert_ids, gate_values, gate_weight, up_weight, down_weight):
    flat = expert_ids.reshape(1, TOK * TOP)
    route = jnp.arange(TOK * TOP)
    same = (flat.reshape(TOK * TOP, 1) == flat) & (route[:, None] < route[None, :])
    rank = jnp.sum(same.astype(jnp.int32), axis=0, keepdims=True)
    code = (flat * 2 + rank).astype(F32)
    gates = gate_values.reshape(1, TOK * TOP)
    hi = lax.reduce_precision(gates, 8, 7)
    meta = jnp.concatenate([code, hi, gates - hi, jnp.zeros((13, TOK * TOP), F32)], axis=0).astype(BF16)

    vmem = pl.BlockSpec(memory_space=pltpu.VMEM)
    hbm = pl.BlockSpec(memory_space=pltpu.HBM)
    dma = pltpu.SemaphoreType.DMA
    v = pltpu.VMEM
    outs = (
        jax.ShapeDtypeStruct((TOK, D), BF16),
        jax.ShapeDtypeStruct((TOK, D), BF16),
        jax.ShapeDtypeStruct((8, 128), F32),
        jax.ShapeDtypeStruct((1, COLS, H), F32),
        jax.ShapeDtypeStruct((1, COLS, H), F32),
    )
    mixed, igrad, gg, ggw, guw = pl.pallas_call(
        kernel,
        out_shape=outs,
        in_specs=[vmem] * 3 + [hbm] * 3,
        out_specs=[vmem] * 5,
        scratch_shapes=[
            v((3, NX, COLS, H), BF16),
            v((NZ, TOK, WIDE), BF16),
            v((NZ, TOK, D), BF16),
            v((2, 2, NJ, 16, D), BF16),
            v((2, 2, NJ, 16, D), BF16),
            v((2, ROWS, D), BF16),
            v((D, 2 * ROWS), BF16),
            v((2 * ROWS, H), F32),
            v((2 * ROWS, H), F32),
            v((2 * ROWS, H), BF16),
            v((2, 2 * ROWS, H), BF16),
            v((2, 2, NJ, 16, D), BF16),
            v((2, 2, NJ, 16, D), BF16),
            v((NZ, TOK, WIDE), F32),
            v((NZ, TOK, D), F32),
            v((NZ, TOK, WIDE), BF16),
            v((NZ, TOK, D), BF16),
            v((NZ, TOK, WIDE), BF16),
            v((NZ, TOK, D), BF16),
            v((2, NX, COLS, H), BF16),
            v((2, NX, COLS, H), BF16),
            v((2, ROWS, ROWS), BF16),
            v((2, 3, ROWS, ROWS), BF16),
            v((2, ROWS, 128), BF16),
            dma((3, NX)), dma((3, NX)), dma((3,)),
            dma((2, NZ)), dma((2, NZ)),
            dma((2, 2, NJ)), dma((2, 2, NJ)),
            dma((2, 2, NJ)), dma((2, 2, NJ)),
            dma((2, NZ)), dma((2, NZ)),
            dma((2, NX)), dma((2, NX)),
        ],
        compiler_params=pltpu.CompilerParams(
            collective_id=0, has_side_effects=True, vmem_limit_bytes=48 * 2**20
        ),
        name="experts",
    )(tokens, cotangent, meta, gate_weight, up_weight, down_weight)
    return mixed, igrad, gg[0].reshape(TOK, TOP), ggw, guw


def solution(mesh):
    token = P(("dp", "expert"), None)
    weight = P("expert", "dp", None)
    return jax.shard_map(
        body,
        mesh=mesh,
        in_specs=(token,) * 4 + (weight,) * 3,
        out_specs=(token,) * 3 + (weight,) * 2,
        check_vma=False,
    )
```

time: 155 us -> 125 us (0.81)
  Pallas kernels: 144 us -> 113 us
    pallas_call x1, Pallas kernels: 144 us -> 113 us  [body(): pl.pallas_call(kernel, out_shape=outs, in_specs=[vmem] * 3 + [hbm] * 3, o...]
where the time goes in v2:
time: 125 us; the launch traced here: 124 us
  Pallas kernels  113 us (90%)
  local copies, waits for them, and re-layouts  9.56 us (8%)
    pallas_call x1, Pallas kernels, body(): pl.pallas_call(kernel, out_shape=outs, in_specs=[vmem] * 3 + [hbm] * 3, o...  113 us
    unnamed x17, local copies, waits for them, and re-layouts  9.05 us

profile of v2, /device:TPU:1, one launch (start us, length us, event | category | flops | bytes accessed | tf_op | source)
XLA Modules:
  0.0 124.3 jit_solution(9582645882253234415)
XLA Ops:
  0.6 0.0 copy-start.3
  0.7 0.1 pad.3.clone
  0.7 0.7 broadcast_multiply_fusion
  1.4 0.1 copy.20
  1.5 0.1 mul.19
  1.6 0.8 copy.22
  2.3 0.1 reshape.70
  2.4 0.8 copy.21
  3.2 0.1 eq.15
  3.3 0.1 convert_reduce_fusion
  3.4 0.1 maximum_maximum_fusion.meta_ref
  3.5 0.0 copy-done.3
  3.5 0.0 copy-start
  3.5 1.0 copy-done
  4.5 0.0 copy-start.1
  4.5 1.0 copy-done.1
  5.5 0.0 copy-start.2
  5.5 1.0 copy-done.2
  6.5 0.0 copy-start.4
  6.5 0.8 copy-done.4
  7.3 113.2 %experts.1 = (bf16[16,2048]{1,0:T(8,128)(2,1)S(1)}, bf16[16,2048]{1,0:T(8,128)(2,1)S(1)}, f32[8,128]{1,0:T(8,128)S(1)}, f32[1,512,384]{2,1,0:T(8,128)S(1)}, f32[1,512,384]{2,1,0:T(8,128)S(1)}) custom-call(bf16[16,2048]{1,0:T(8,128)(2,1)S(1)} %copy-done.3, bf16[16,2048]{1,0:T(8,128)(2,1)S(1)} %copy-done.4, bf16[16,128]{1,0:T(8,128)(2,1)S(1)} %maximum_maximum_fusion.meta_ref, ...), custom_call_target="tpu_custom_call" | custom-call | tf_op jit(solution)/shard_map/experts/pallas_call | solution.py:363
  120.5 0.1 reshape_squeeze.3
  120.6 0.7 copy.23
  121.3 0.6 copy.28
  121.9 0.6 copy.29
  122.5 0.9 copy.30
  123.4 0.9 copy.31
  (4 shorter events, 0.0 us)
Async XLA Ops:
  0.6 2.9 %copy-start.3 = (bf16[16,2048]{1,0:T(8,128)(2,1)S(1)}, bf16[16,2048]{1,0:T(8,128)(2,1)}, u32[]{:S(2)}) copy-start(bf16[16,2048]{1,0:T(8,128)(2,1)} %tok_ref.1) | copy-start | bytes 196612
  3.5 1.0 copy-start
  4.5 1.0 copy-start.1
  5.5 1.0 copy-start.2
  6.5 0.8 copy-start.4

commit v3 on v2

v3 whole, which is shorter than its diff:
```python
import functools

import jax
import jax.numpy as jnp
from jax import lax
from jax.experimental import pallas as pl
from jax.experimental.pallas import tpu as pltpu
from jax.sharding import PartitionSpec as P

MESH = pl.DeviceIdType.MESH
NX, NZ, NJ = 4, 16, 8
TOK, D, H, TOP = 16, 2048, 384, 8
NB = 8
ROWS = NB * TOK
COLS = 512
WIDE = D + 128
F32, BF16 = jnp.float32, jnp.bfloat16
NT = (((1,), (1,)), ((), ()))


def dot(a, b):
    return jnp.dot(a, b, preferred_element_type=F32)


def dot_t(a, b):
    return lax.dot_general(a, b, NT, preferred_element_type=F32)


def iota(shape, dim):
    return lax.broadcasted_iota(jnp.int32, shape, dim)


def halves(v):
    hi = v.astype(BF16)
    return hi, (v - hi.astype(F32)).astype(BF16)


def kernel(
    tok_ref, cot_ref, ids_ref, gates_ref, gw_ref, uw_ref, dw_ref,
    mixed_ref, igrad_ref, gg_ref, ggw_ref, guw_ref,
    W, AGT, AGC, STG, ROW, PCOT, XS, XT, HG, HU, ACT, DGU, OST, RET, PARTM, PARTX, RSSM, RSSX, RSRM, RSRX, ONE, TG, EX, WG, TO,
    w_s, w_r, l_s, ag_s, ag_r, di_s, di_r, re_s, re_r, rs_s, rs_r, xs_s, xs_r, dg_s, dg_r,
):
    x = lax.axis_index("dp")
    e = lax.axis_index("expert")
    z = e // NJ
    j = lax.rem(e, NJ)

    def zpeer(d):
        return {"dp": x, "expert": lax.rem(z + d + NZ, NZ) * NJ + j}

    def jat(q):
        return lax.rem(j + q + NJ, NJ)

    def xat(q):
        return lax.rem(x + q + NX, NX)

    def jpeer(q):
        return {"dp": x, "expert": z * NJ + jat(q)}

    def xpeer(q):
        return {"dp": xat(q), "expert": e}

    def local(src, dst, sem):
        copy = pltpu.make_async_copy(src, dst, sem)
        copy.start()
        return copy

    first = [local(tok_ref, AGT.at[4, :, pl.ds(0, D)], l_s.at[3]), local(cot_ref, AGC.at[4], l_s.at[4])]
    own = [local(ref.at[0], W.at[i, x], l_s.at[i]) for i, ref in enumerate((gw_ref, uw_ref, dw_ref))]

    barrier = pltpu.get_barrier_semaphore()
    peers = [zpeer(d) for d in (1, -1)] + [jpeer(q) for q in range(1, NJ)] + [xpeer(q) for q in range(1, NX)]
    for peer in peers:
        pl.semaphore_signal(barrier, inc=1, device_id=peer, device_id_type=MESH)

    spread = (lax.rem(iota((TOK, 128), 1), TOK) == iota((TOK, 128), 0)).astype(F32)
    here = iota((TOP, 128), 1) // TOK == iota((TOP, 128), 0)

    def flat(v):
        return jnp.sum(jnp.where(here, dot(v, spread), 0.0), axis=0, keepdims=True)

    ids = flat(ids_ref[...].astype(F32))
    hi, lo = halves(gates_ref[...])
    table = jnp.broadcast_to(ids, (128, 128))
    again = (table == table.T) & (iota((128, 128), 0) < iota((128, 128), 1))
    code = ids * 2.0 + jnp.sum(again.astype(F32), axis=0, keepdims=True)
    row = iota((TOK, 128), 0)
    meta = jnp.where(row == 0, code, jnp.where(row == 1, flat(hi.astype(F32)), jnp.where(row == 2, flat(lo.astype(F32)), 0.0)))
    AGT[4, :, D:] = meta.astype(BF16)
    pl.semaphore_wait(barrier, len(peers))

    sent = []

    def send(src, dst, s, r, peer):
        copy = pltpu.make_async_remote_copy(
            src_ref=src, dst_ref=dst, send_sem=s, recv_sem=r, device_id=peer, device_id_type=MESH
        )
        copy.start()
        sent.append(copy)
        return copy

    AG = (AGT, AGC)
    arrive = {}

    CUT = D // 2
    PIECES = ((pl.ds(0, CUT), pl.ds(CUT, WIDE - CUT)), (pl.ds(0, CUT), pl.ds(CUT, D - CUT)))

    def ag_send(tc, half, r, step):
        to = (r - step) % NZ
        at = PIECES[tc][half]
        arrive[tc, half, to] = send(
            AG[tc].at[r, :, at], AG[tc].at[to, :, at], ag_s.at[tc, half, to], ag_r.at[tc, half, to], zpeer(step)
        )

    def ring(h):
        for tc in (0, 1):
            if h == 0:
                first[tc].wait()
            for half in (0, 1):
                if h > 0:
                    arrive[tc, half, (4 - h) % NZ].wait_recv()
                if h < 8:
                    ag_send(tc, half, (4 - h) % NZ, 1)
                if 0 < h < 8:
                    arrive[tc, half, 4 + h].wait_recv()
                if h < 7:
                    ag_send(tc, half, 4 + h, -1)

    HALF = COLS // 2
    weights = {}
    relays = {}

    def weight_out(i):
        ref = (gw_ref, uw_ref, dw_ref)[i]
        for q in (1, 3):
            weights[i, q] = send(ref.at[0], W.at[i, x], w_s.at[i, q], w_r.at[i, q], xpeer(q))

    def relay(i):
        for q, half in ((1, 0), (3, 1)):
            weights[i, q].wait_recv()
            block = W.at[i, xat(-q), pl.ds(half * HALF, HALF)]
            relays[i, half] = send(block, block, w_s.at[i, 2 * half], w_r.at[i, 2 * half], xpeer(q))

    def select(ch):
        m = AGT[pl.ds(NB * ch, NB), :, D:].reshape(ROWS, 128)
        row, col = iota((ROWS, ROWS), 0), iota((ROWS, ROWS), 1)
        mine = lax.rem(row, 16) // 2 * TOK
        codes = dot((col == mine).astype(F32).astype(BF16), m)
        gates = dot(((col == mine + 1) | (col == mine + 2)).astype(F32).astype(BF16), m)
        row = iota((ROWS, 128), 0)
        col = iota((ROWS, 128), 1)
        want = ((z * NJ + row // 16) * 2 + lax.rem(row, 2)).astype(F32)
        taken = (codes == want).astype(F32)
        gate = jnp.sum(taken * gates, axis=1, keepdims=True)
        fold = (lax.rem(row, TOK) == lax.rem(col, TOK)).astype(F32).astype(BF16)
        one = dot(taken.astype(BF16), fold)
        one = jnp.where(lax.rem(row, 16) // 2 == col // TOK, one, 0.0)
        EX[ch] = taken.astype(BF16)
        ONE[ch] = one.astype(BF16)
        one_t = one.T
        TG[ch, 0] = one_t.astype(BF16)
        gated = (one * gate).T
        hi, lo = halves(gated)
        TG[ch, 1] = hi
        TG[ch, 2] = lo
        return gate

    rows_in = {}

    def pack(tc, ch, gate):
        one = ONE[ch]

        @pl.loop(0, D // COLS)
        def _(n):
            at = pl.ds(pl.multiple_of(n * COLS, COLS), COLS)
            picked = dot(one, AG[tc][pl.ds(NB * ch, NB), :, at].reshape(ROWS, COLS))
            if tc == 1:
                PCOT[ch, :, at] = picked.astype(BF16)
                picked = picked * gate
            STG[ch, tc, :, :, at] = picked.astype(BF16).reshape(NJ, 16, COLS)

        for q in range(1, NJ):
            rows_in[ch, tc, q] = send(
                STG.at[ch, tc, jat(q)], ROW.at[tc, ch, j], di_s.at[ch, tc, q], di_r.at[ch, tc, q], jpeer(q)
            )
        ROW[tc, ch, j] = STG[ch, tc, j]

    def rows_wait(tc):
        for ch in (0, 1):
            for q in range(1, NJ):
                rows_in[ch, tc, q].wait_recv()

    ring(0)
    weight_out(0)
    weight_out(1)
    ring(1)
    ring(2)
    ring(3)
    weight_out(2)
    ring(4)
    gate_a = select(0)
    pack(0, 0, gate_a)
    ring(5)
    pack(1, 0, gate_a)
    relay(0)
    relay(1)
    ring(6)
    ring(7)
    relay(2)
    ring(8)
    gate_b = select(1)
    pack(0, 1, gate_b)
    pack(1, 1, gate_b)
    rows_wait(0)

    slices = []
    for q in (2, 1, 3):
        at = pl.ds(pl.multiple_of(xat(q) * COLS, COLS), COLS)
        slices.append(send(ROW.at[0, :, :, :, at], XS.at[x], xs_s.at[q], xs_r.at[q], xpeer(q)))
    XS[x] = ROW[0, :, :, :, pl.ds(pl.multiple_of(x * COLS, COLS), COLS)]

    def weight_in(i):
        own[i].wait()
        for half in (0, 1):
            relays[i, half].wait_recv()

    def rows_by(i, tc, to):
        to[...] = jnp.zeros_like(to)

        @pl.loop(0, NX)
        def _(n):
            at = pl.ds(pl.multiple_of(n * COLS, COLS), COLS)
            to[...] += dot(ROW[tc, :, :, :, at].reshape(2 * ROWS, COLS), W[i, n])

    weight_in(0)
    rows_by(0, 0, HG)
    weight_in(1)
    rows_by(1, 0, HU)
    hg, hu = HG[...], HU[...]
    sigma = jax.nn.sigmoid(hg)
    ACT[...] = (hg * sigma * hu).astype(BF16)
    weight_in(2)

    back = {}

    def give_back(arr, ch):
        for q in range(1, NJ):
            back[arr, ch, q] = send(
                OST.at[arr, ch, jat(q)], RET.at[arr, ch, j], re_s.at[arr, ch, q], re_r.at[arr, ch, q], jpeer(q)
            )
        RET[arr, ch, j] = OST[arr, ch, j]

    @pl.loop(0, NX)
    def _(n):
        at = pl.ds(pl.multiple_of(n * COLS, COLS), COLS)
        OST[0, :, :, :, at] = dot_t(ACT[...], W[2, n]).astype(BF16).reshape(2, NJ, 16, COLS)

    PART, RSS, RSR = (PARTM, PARTX), (RSSM, RSSX), (RSRM, RSRX)

    def combine(arr, ch):
        for q in range(1, NJ):
            back[arr, ch, q].wait_recv()

        def step(n, dots):
            at = pl.ds(pl.multiple_of(n * COLS, COLS), COLS)
            block = RET[arr, ch, :, :, at].reshape(ROWS, COLS)
            if arr == 0:
                part = dot(TG[ch, 1], block) + dot(TG[ch, 2], block)
                dots = dots + jnp.sum(block.astype(F32) * PCOT[ch, :, at].astype(F32), axis=1, keepdims=True)
            else:
                part = dot(TG[ch, 0], block)
            PART[arr][pl.ds(NB * ch, NB), :, at] = part.reshape(NB, TOK, COLS)
            return dots

        dots = lax.fori_loop(0, D // COLS, step, jnp.zeros((ROWS, 1), F32))
        if arr == 0:
            hi, lo = halves(EX[ch].astype(F32) * dots)
            row, col = iota((ROWS, ROWS), 0), iota((ROWS, ROWS), 1)
            first = lax.rem(col, 16) // 2 * TOK
            grads = dot((row == first).astype(F32).astype(BF16), hi) + dot((row == first + 1).astype(F32).astype(BF16), lo)
            PARTM[pl.ds(NB * ch, NB), :, D:] = grads.reshape(NB, TOK, 128)

    arrived = {}

    def rs_sum(arr, half, r, *others):
        at = PIECES[arr][half]
        value = PART[arr][r, :, at]
        for other in others:
            arrived[arr, half, other].wait_recv()
            value = value + RSR[arr][other, :, at].astype(F32)
        return value

    def rs_send(arr, r, step, *others):
        for half in (0, 1):
            at = PIECES[arr][half]
            RSS[arr][r, :, at] = rs_sum(arr, half, r, *others).astype(BF16)
            arrived[arr, half, r] = send(
                RSS[arr].at[r, :, at], RSR[arr].at[r, :, at], rs_s.at[arr, half, r], rs_r.at[arr, half, r], zpeer(step)
            )

    def hop(arr, h):
        r = (12 + h) % NZ
        rs_send(arr, r, -1, *(((r - 1) % NZ,) if h else ()))
        if h < 7:
            rs_send(arr, 11 - h, 1, *((12 - h,) if h else ()))

    give_back(0, 1)
    rows_wait(1)
    rows_by(2, 1, HU)
    da = HU[...]
    DGU[x, 1] = (da * hg * sigma).astype(BF16)
    DGU[x, 0] = (da * hu * sigma * (1.0 + hg * (1.0 - sigma))).astype(BF16)
    grads = [send(DGU.at[x], DGU.at[x], dg_s.at[q], dg_r.at[q], xpeer(q)) for q in (2, 1, 3)]

    @pl.loop(0, NX)
    def _(n):
        at = pl.ds(pl.multiple_of(n * COLS, COLS), COLS)
        dx = dot_t(DGU[x, 0], W[0, n]) + dot_t(DGU[x, 1], W[1, n])
        OST[1, :, :, :, at] = dx.astype(BF16).reshape(2, NJ, 16, COLS)

    give_back(1, 1)
    give_back(0, 0)
    give_back(1, 0)
    combine(0, 1)
    hop(0, 0)
    combine(1, 1)
    hop(1, 0)
    hop(0, 1)
    for copy in slices:
        copy.wait_recv()

    @pl.loop(0, NX)
    def _(n):
        XT[n] = XS[n].reshape(2 * ROWS, COLS).T

    hop(1, 1)
    hop(0, 2)
    hop(1, 2)
    hop(0, 3)
    combine(0, 0)
    hop(1, 3)
    hop(0, 4)
    combine(1, 0)
    for h in (4, 5, 6):
        hop(1, h)
        hop(0, h + 1)
    hop(1, 7)
    for copy in grads:
        copy.wait_recv()
    WG[...] = jnp.zeros_like(WG)

    @pl.loop(0, NX)
    def _(n):
        WG[0] += dot(XT[n], DGU[n, 0])
        WG[1] += dot(XT[n], DGU[n, 1])

    out = [local(WG.at[0], ggw_ref.at[0], l_s.at[5]), local(WG.at[1], guw_ref.at[0], l_s.at[6])]
    TO[0, :, :CUT] = rs_sum(0, 0, 4, 3, 5).astype(BF16)
    total = rs_sum(0, 1, 4, 3, 5)
    TO[0, :, CUT:] = total[:, : D - CUT].astype(BF16)
    total = total[:, D - CUT :]
    out.append(local(TO.at[0], mixed_ref, l_s.at[7]))
    mine = jnp.where(iota((TOK, 128), 1) // TOK == row, total[0:1] + total[1:2], 0.0)
    hi, lo = halves(mine)
    unfold = (lax.rem(iota((128, TOK), 0), TOK) == iota((128, TOK), 1)).astype(F32).astype(BF16)
    gg_ref[...] = (dot(hi, unfold) + dot(lo, unfold))[:TOP]
    TO[1, :, :CUT] = rs_sum(1, 0, 4, 3, 5).astype(BF16)
    TO[1, :, CUT:] = rs_sum(1, 1, 4, 3, 5).astype(BF16)
    out.append(local(TO.at[1], igrad_ref, l_s.at[8]))
    for copy in sent:
        copy.wait_send()
    for copy in out:
        copy.wait()


def body(tokens, cotangent, expert_ids, gate_values, gate_weight, up_weight, down_weight):
    vmem = pl.BlockSpec(memory_space=pltpu.VMEM)
    hbm = pl.BlockSpec(memory_space=pltpu.HBM)
    dma = pltpu.SemaphoreType.DMA
    v = pltpu.VMEM
    outs = (
        jax.ShapeDtypeStruct((TOK, D), BF16),
        jax.ShapeDtypeStruct((TOK, D), BF16),
        jax.ShapeDtypeStruct((TOP, TOK), F32),
        jax.ShapeDtypeStruct((1, COLS, H), F32),
        jax.ShapeDtypeStruct((1, COLS, H), F32),
    )
    mixed, igrad, gg, ggw, guw = pl.pallas_call(
        kernel,
        out_shape=outs,
        in_specs=[hbm] * 2 + [vmem] * 2 + [hbm] * 3,
        out_specs=[hbm] * 2 + [vmem] + [hbm] * 2,
        scratch_shapes=[
            v((3, NX, COLS, H), BF16),
            v((NZ, TOK, WIDE), BF16),
            v((NZ, TOK, D), BF16),
            v((2, 2, NJ, 16, D), BF16),
            v((2, 2, NJ, 16, D), BF16),
            v((2, ROWS, D), BF16),
            v((NX, 2, NJ, 16, COLS), BF16),
            v((NX, COLS, 2 * ROWS), BF16),
            v((2 * ROWS, H), F32),
            v((2 * ROWS, H), F32),
            v((2 * ROWS, H), BF16),
            v((NX, 2, 2 * ROWS, H), BF16),
            v((2, 2, NJ, 16, D), BF16),
            v((2, 2, NJ, 16, D), BF16),
            v((NZ, TOK, WIDE), F32),
            v((NZ, TOK, D), F32),
            v((NZ, TOK, WIDE), BF16),
            v((NZ, TOK, D), BF16),
            v((NZ, TOK, WIDE), BF16),
            v((NZ, TOK, D), BF16),
            v((2, ROWS, ROWS), BF16),
            v((2, 3, ROWS, ROWS), BF16),
            v((2, ROWS, 128), BF16),
            v((2, COLS, H), F32),
            v((2, TOK, D), BF16),
            dma((3, NX)), dma((3, NX)), dma((9,)),
            dma((2, 2, NZ)), dma((2, 2, NZ)),
            dma((2, 2, NJ)), dma((2, 2, NJ)),
            dma((2, 2, NJ)), dma((2, 2, NJ)),
            dma((2, 2, NZ)), dma((2, 2, NZ)),
            dma((NX,)), dma((NX,)),
            dma((NX,)), dma((NX,)),
        ],
        compiler_params=pltpu.CompilerParams(
            collective_id=0, has_side_effects=True, vmem_limit_bytes=60 * 2**20
        ),
        name="experts",
    )(tokens, cotangent, expert_ids.T, gate_values.T, gate_weight, up_weight, down_weight)
    return mixed, igrad, gg.T, ggw, guw


def solution(mesh):
    token = P(("dp", "expert"), None)
    weight = P("expert", "dp", None)
    return jax.shard_map(
        body,
        mesh=mesh,
        in_specs=(token,) * 4 + (weight,) * 3,
        out_specs=(token,) * 3 + (weight,) * 2,
        check_vma=False,
    )
```

time: 125 us -> 109 us (0.87)
  Pallas kernels: 113 us -> 101 us
  local copies, waits for them, and re-layouts: 9.56 us -> 5.8 us
    pallas_call x1, Pallas kernels: 113 us -> 101 us  [body(): pl.pallas_call(kernel, out_shape=outs, in_specs=[hbm] * 2 + [vmem] * 2 +...]
    unnamed x17 -> x11, local copies, waits for them, and re-layouts: 9.05 us -> 5.8 us
where the time goes in v3:
time: 109 us; the launch traced here: 107 us
  Pallas kernels  101 us (93%)
  local copies, waits for them, and re-layouts  5.8 us (5%)
    pallas_call x1, Pallas kernels, body(): pl.pallas_call(kernel, out_shape=outs, in_specs=[hbm] * 2 + [vmem] * 2 +...  101 us
    unnamed x11, local copies, waits for them, and re-layouts  5.8 us

profile of v3, /device:TPU:1, one launch (start us, length us, event | category | flops | bytes accessed | tf_op | source)
XLA Modules:
  0.0 107.1 jit_solution(15668983315055088791)
XLA Ops:
  0.6 100.6 %experts.1 = (bf16[16,2048]{1,0:T(8,128)(2,1)}, bf16[16,2048]{1,0:T(8,128)(2,1)}, f32[8,16]{1,0:T(8,128)}, f32[1,512,384]{2,1,0:T(8,128)}, f32[1,512,384]{2,1,0:T(8,128)}) custom-call(bf16[16,2048]{1,0:T(8,128)(2,1)} %tok_ref.1, bf16[16,2048]{1,0:T(8,128)(2,1)} %cot_ref.1, s32[8,16]{1,0:T(8,128)} %bitcast.3, f32[8,16]{1,0:T(8,128)} %bitcast.4, ...), custom_call_target="tpu_custom_call" | custom-call | tf_op jit(solution)/shard_map/experts/pallas_call | solution.py:389
  101.3 0.0 copy-start.1
  101.3 1.5 %copy.17 = bf16[16,2048]{1,0:T(8,128)(2,1)} copy(bf16[16,2048]{1,0:T(8,128)(2,1)} %get-tuple-element.20) | data formatting | bytes 131072
  102.8 0.0 copy-done.1
  102.8 0.0 copy-start.2
  102.8 0.6 copy.18
  103.4 0.0 copy-done.2
  103.5 0.6 copy.19
  104.1 0.0 copy-start
  104.1 2.1 %copy.20 = f32[1,512,384]{2,1,0:T(8,128)} copy(f32[1,512,384]{2,1,0:T(8,128)} %get-tuple-element.23) | data formatting | bytes 1572864
  106.2 0.0 copy-done
  106.2 0.9 copy.21
Async XLA Ops:
  101.3 1.5 %copy-start.1 = (bf16[16,2048]{1,0:T(8,128)(2,1)S(1)}, bf16[16,2048]{1,0:T(8,128)(2,1)}, u32[]{:S(2)}) copy-start(bf16[16,2048]{1,0:T(8,128)(2,1)} %get-tuple-element.21) | copy-start | bytes 196612
  102.8 0.7 copy-start.2
  104.1 2.1 %copy-start = (f32[1,512,384]{2,1,0:T(8,128)S(1)}, f32[1,512,384]{2,1,0:T(8,128)}, u32[]{:S(2)}) copy-start(f32[1,512,384]{2,1,0:T(8,128)} %get-tuple-element.24) | copy-start | bytes 2359300

commit v4 on v3

--- a/solution.py
+++ b/solution.py
@@ -13,6 +13,7 @@
 NB = 8
 ROWS = NB * TOK
 COLS = 512
+SPLIT = 2
 WIDE = D + 128
 F32, BF16 = jnp.float32, jnp.bfloat16
 NT = (((1,), (1,)), ((), ()))
@@ -37,7 +38,7 @@
 
 def kernel(
     tok_ref, cot_ref, ids_ref, gates_ref, gw_ref, uw_ref, dw_ref,
-    mixed_ref, igrad_ref, gg_ref, ggw_ref, guw_ref,
+    token_out, gg_ref, weight_out_ref,
     W, AGT, AGC, STG, ROW, PCOT, XS, XT, HG, HU, ACT, DGU, OST, RET, PARTM, PARTX, RSSM, RSSX, RSRM, RSRX, ONE, TG, EX, WG, TO,
     w_s, w_r, l_s, ag_s, ag_r, di_s, di_r, re_s, re_r, rs_s, rs_r, xs_s, xs_r, dg_s, dg_r,
 ):
@@ -103,8 +104,9 @@
     AG = (AGT, AGC)
     arrive = {}
 
-    CUT = D // 2
-    PIECES = ((pl.ds(0, CUT), pl.ds(CUT, WIDE - CUT)), (pl.ds(0, CUT), pl.ds(CUT, D - CUT)))
+    CUT = D // SPLIT
+    LAST = D - CUT
+    PIECES = [[pl.ds(i * CUT, CUT) for i in range(SPLIT - 1)] + [pl.ds(LAST, end - LAST)] for end in (WIDE, D)]
 
     def ag_send(tc, half, r, step):
         to = (r - step) % NZ
@@ -117,7 +119,7 @@
         for tc in (0, 1):
             if h == 0:
                 first[tc].wait()
-            for half in (0, 1):
+            for half in range(SPLIT):
                 if h > 0:
                     arrive[tc, half, (4 - h) % NZ].wait_recv()
                 if h < 8:
@@ -251,11 +253,6 @@
             )
         RET[arr, ch, j] = OST[arr, ch, j]
 
-    @pl.loop(0, NX)
-    def _(n):
-        at = pl.ds(pl.multiple_of(n * COLS, COLS), COLS)
-        OST[0, :, :, :, at] = dot_t(ACT[...], W[2, n]).astype(BF16).reshape(2, NJ, 16, COLS)
-
     PART, RSS, RSR = (PARTM, PARTX), (RSSM, RSSX), (RSRM, RSRX)
 
     def combine(arr, ch):
@@ -292,7 +289,7 @@
         return value
 
     def rs_send(arr, r, step, *others):
-        for half in (0, 1):
+        for half in range(SPLIT):
             at = PIECES[arr][half]
             RSS[arr][r, :, at] = rs_sum(arr, half, r, *others).astype(BF16)
             arrived[arr, half, r] = send(
@@ -305,6 +302,24 @@
         if h < 7:
             rs_send(arr, 11 - h, 1, *((12 - h,) if h else ()))
 
+    def outputs(ch):
+        half = slice(ch * ROWS, ch * ROWS + ROWS)
+
+        @pl.loop(0, NX)
+        def _(n):
+            at = pl.ds(pl.multiple_of(n * COLS, COLS), COLS)
+            OST[0, ch, :, :, at] = dot_t(ACT[half], W[2, n]).astype(BF16).reshape(NJ, 16, COLS)
+
+    def input_grads(ch):
+        half = slice(ch * ROWS, ch * ROWS + ROWS)
+
+        @pl.loop(0, NX)
+        def _(n):
+            at = pl.ds(pl.multiple_of(n * COLS, COLS), COLS)
+            dx = dot_t(DGU[x, 0, half], W[0, n]) + dot_t(DGU[x, 1, half], W[1, n])
+            OST[1, ch, :, :, at] = dx.astype(BF16).reshape(NJ, 16, COLS)
+
+    outputs(1)
     give_back(0, 1)
     rows_wait(1)
     rows_by(2, 1, HU)
@@ -313,14 +328,11 @@
     DGU[x, 0] = (da * hu * sigma * (1.0 + hg * (1.0 - sigma))).astype(BF16)
     grads = [send(DGU.at[x], DGU.at[x], dg_s.at[q], dg_r.at[q], xpeer(q)) for q in (2, 1, 3)]
 
-    @pl.loop(0, NX)
-    def _(n):
-        at = pl.ds(pl.multiple_of(n * COLS, COLS), COLS)
-        dx = dot_t(DGU[x, 0], W[0, n]) + dot_t(DGU[x, 1], W[1, n])
-        OST[1, :, :, :, at] = dx.astype(BF16).reshape(2, NJ, 16, COLS)
-
+    input_grads(1)
     give_back(1, 1)
+    outputs(0)
     give_back(0, 0)
+    input_grads(0)
     give_back(1, 0)
     combine(0, 1)
     hop(0, 0)
@@ -355,19 +367,20 @@
         WG[0] += dot(XT[n], DGU[n, 0])
         WG[1] += dot(XT[n], DGU[n, 1])
 
-    out = [local(WG.at[0], ggw_ref.at[0], l_s.at[5]), local(WG.at[1], guw_ref.at[0], l_s.at[6])]
-    TO[0, :, :CUT] = rs_sum(0, 0, 4, 3, 5).astype(BF16)
-    total = rs_sum(0, 1, 4, 3, 5)
-    TO[0, :, CUT:] = total[:, : D - CUT].astype(BF16)
-    total = total[:, D - CUT :]
-    out.append(local(TO.at[0], mixed_ref, l_s.at[7]))
+    out = [local(WG, weight_out_ref, l_s.at[5])]
+    for i in range(SPLIT - 1):
+        TO[0, :, PIECES[0][i]] = rs_sum(0, i, 4, 3, 5).astype(BF16)
+    total = rs_sum(0, SPLIT - 1, 4, 3, 5)
+    TO[0, :, LAST:] = total[:, :CUT].astype(BF16)
+    total = total[:, CUT:]
+    out.append(local(TO.at[0], token_out.at[0], l_s.at[6]))
     mine = jnp.where(iota((TOK, 128), 1) // TOK == row, total[0:1] + total[1:2], 0.0)
     hi, lo = halves(mine)
     unfold = (lax.rem(iota((128, TOK), 0), TOK) == iota((128, TOK), 1)).astype(F32).astype(BF16)
     gg_ref[...] = (dot(hi, unfold) + dot(lo, unfold))[:TOP]
-    TO[1, :, :CUT] = rs_sum(1, 0, 4, 3, 5).astype(BF16)
-    TO[1, :, CUT:] = rs_sum(1, 1, 4, 3, 5).astype(BF16)
-    out.append(local(TO.at[1], igrad_ref, l_s.at[8]))
+    for i in range(SPLIT):
+        TO[1, :, PIECES[1][i]] = rs_sum(1, i, 4, 3, 5).astype(BF16)
+    out.append(local(TO.at[1], token_out.at[1], l_s.at[7]))
     for copy in sent:
         copy.wait_send()
     for copy in out:
@@ -380,17 +393,15 @@
     dma = pltpu.SemaphoreType.DMA
     v = pltpu.VMEM
     outs = (
-        jax.ShapeDtypeStruct((TOK, D), BF16),
-        jax.ShapeDtypeStruct((TOK, D), BF16),
+        jax.ShapeDtypeStruct((2, TOK, D), BF16),
         jax.ShapeDtypeStruct((TOP, TOK), F32),
-        jax.ShapeDtypeStruct((1, COLS, H), F32),
-        jax.ShapeDtypeStruct((1, COLS, H), F32),
+        jax.ShapeDtypeStruct((2, COLS, H), F32),
     )
-    mixed, igrad, gg, ggw, guw = pl.pallas_call(
+    token_grads, gg, weight_grads = pl.pallas_call(
         kernel,
         out_shape=outs,
         in_specs=[hbm] * 2 + [vmem] * 2 + [hbm] * 3,
-        out_specs=[hbm] * 2 + [vmem] + [hbm] * 2,
+        out_specs=[hbm, vmem, hbm],
         scratch_shapes=[
             v((3, NX, COLS, H), BF16),
             v((NZ, TOK, WIDE), BF16),
@@ -417,11 +428,11 @@
             v((2, ROWS, 128), BF16),
             v((2, COLS, H), F32),
             v((2, TOK, D), BF16),
-            dma((3, NX)), dma((3, NX)), dma((9,)),
-            dma((2, 2, NZ)), dma((2, 2, NZ)),
+            dma((3, NX)), dma((3, NX)), dma((8,)),
+            dma((2, SPLIT, NZ)), dma((2, SPLIT, NZ)),
             dma((2, 2, NJ)), dma((2, 2, NJ)),
             dma((2, 2, NJ)), dma((2, 2, NJ)),
-            dma((2, 2, NZ)), dma((2, 2, NZ)),
+            dma((2, SPLIT, NZ)), dma((2, SPLIT, NZ)),
             dma((NX,)), dma((NX,)),
             dma((NX,)), dma((NX,)),
         ],
@@ -430,7 +441,7 @@
         ),
         name="experts",
     )(tokens, cotangent, expert_ids.T, gate_values.T, gate_weight, up_weight, down_weight)
-    return mixed, igrad, gg.T, ggw, guw
+    return token_grads[0], token_grads[1], gg.T, weight_grads[:1], weight_grads[1:]
 
 
 def solution(mesh):

time: 109 us -> 107 us (0.982)
    unnamed x11 -> x3, local copies, waits for them, and re-layouts: 5.8 us -> 0.6 us
    slice x0 -> x1, local copies, waits for them, and re-layouts: none -> 2.61 us  [body(): weight_grads[1:]]
    squeeze x0 -> x1, local copies, waits for them, and re-layouts: none -> 1.53 us  [body(): token_grads[1]]
where the time goes in v4:
time: 107 us; the launch traced here: 106 us
  Pallas kernels  100 us (93%)
  local copies, waits for them, and re-layouts  4.73 us (4%)
    pallas_call x1, Pallas kernels, body(): pl.pallas_call(kernel, out_shape=outs, in_specs=[hbm] * 2 + [vmem] * 2 +...  100 us
    slice x1, local copies, waits for them, and re-layouts, body(): weight_grads[1:]  2.61 us

profile of v4, /device:TPU:1, one launch (start us, length us, event | category | flops | bytes accessed | tf_op | source)
XLA Modules:
  0.0 105.8 jit_solution(13434983199734871195)
XLA Ops:
  0.6 100.4 %experts.1 = (bf16[2,16,2048]{2,1,0:T(8,128)(2,1)}, f32[8,16]{1,0:T(8,128)}, f32[2,512,384]{2,1,0:T(8,128)}) custom-call(bf16[16,2048]{1,0:T(8,128)(2,1)} %tok_ref.1, bf16[16,2048]{1,0:T(8,128)(2,1)} %cot_ref.1, s32[8,16]{1,0:T(8,128)} %bitcast.7, f32[8,16]{1,0:T(8,128)} %bitcast.8, bf16[1,512,384]{2,1,0:T(8,128)(2,1)} %gw_ref.1, ...), custom_call_target="tpu_custom_call" | custom-call | tf_op jit(solution)/shard_map/experts/pallas_call | solution.py:400
  101.1 1.5 %slice_bitcast_fusion = (bf16[16,2048]{1,0:T(8,128)(2,1)}, bf16[16,2048]{1,0:T(8,128)(2,1)}) fusion(bf16[2,16,2048]{2,1,0:T(8,128)(2,1)} %get-tuple-element.8), kind=kLoop, calls=%fused_computation | loop fusion | bytes 262144 | tf_op jit(solution)/shard_map/squeeze | solution.py:444
  102.6 0.0 copy-start
  102.6 2.6 %fusion = (f32[1,512,384]{2,1,0:T(8,128)}, f32[1,512,384]{2,1,0:T(8,128)}) fusion(f32[2,512,384]{2,1,0:T(8,128)} %get-tuple-element.10), kind=kLoop, calls=%fused_computation.2 | loop fusion | bytes 3145728 | tf_op jit(solution)/shard_map/slice | solution.py:444
  105.2 0.0 copy-done
  105.2 0.6 copy.13
Async XLA Ops:
  102.6 2.6 %copy-start = (f32[8,16]{1,0:T(8,128)S(1)}, f32[8,16]{1,0:T(8,128)}, u32[]{:S(2)}) copy-start(f32[8,16]{1,0:T(8,128)} %get-tuple-element.9) | copy-start | bytes 1540
